TPU v7x, 32 devices: a whole 2x2x4 slice. The times are simulated.
32 devices in a mesh: grp: 4 (over x, core), dp: 8 (over z, y).
Axes of the slice: x: 2, y: 2, z: 4, core: 2. Of those that a mesh axis runs over, the one named last changes fastest.
Arguments:
- images: float32 [2, 64, 3, 32, 32], P(None, ('grp', 'dp')), may hold values from -1 to 1
- noise: float32 [2, 64, 3, 32, 32], P(None, ('grp', 'dp')), may hold values from -4 to 4
- timesteps: int32 [2, 64], P(None, ('grp', 'dp')), may hold values from 16 to 64
- counts: int32 [32, 2], P(('grp', 'dp')), may hold values from 1 to 2, as said below
- teacher: bfloat16 [2239488], replicated
- params: float32 [2239488], replicated
- first_moment: float32 [4, 2239488], P('grp'), may hold values from -5.722046e-06 to 5.722046e-06
- second_moment: float32 [4, 2239488], P('grp'), may hold values from 5.581633e-15 to 8.9306126e-14
- outer_momentum: float32 [2239488], replicated, may hold values from -0.15625 to 0.15625
Outputs:
- new_weights: float32 [2239488], replicated
- new_first: float32 [4, 2239488], P('grp')
- new_second: float32 [4, 2239488], P('grp')
- average_diff: float32 [2239488], replicated
- new_outer: float32 [2239488], replicated
- loss_sum: float32 [4], P('grp')
- loss_count: float32 [4], P('grp')
- grad_norm: float32 [4], P('grp')
Inputs may be any that keep to these rules, and one draw needn't show every extreme that they name: Slots 0 to counts - 1 of a device in a turn hold images; the others are ignored.
All inputs are finite; a program needn't handle non-finite values.
Results may differ from a plain program's by a relative error of at most 0.0083.
Values may be sent and summed in bfloat16 or wider, within the bound.
A program may use at most 512 MiB of HBM per device.

v0:
```python
import math
from types import SimpleNamespace

import jax
import jax.numpy as jnp
from jax import lax
from jax.experimental import pallas as pl
from jax.experimental.pallas import tpu as pltpu
from jax.sharding import PartitionSpec as P

BASE = 128
WIDE = 256
TEMB = 512
FREQ = 128
GROUPS = 32
STEPS = 64
STEP_COUNT = 10

BETA_ONE = 0.9
BETA_TWO = 0.999
EPSILON = 1e-08
RATE_INNER = 0.03
WEIGHT_DECAY = 0.01
CLIP_NORM = 0.005
OUTER_RATE = 0.7
MOMENTUM_OUTER = 0.9

F32 = jnp.float32
BF16 = jnp.bfloat16
LANES = 128
HALF = 16
PIX = HALF * HALF
VMEM_LIMIT = 60 * 1024 * 1024
MESH = pl.DeviceIdType.MESH
PIECES = 5
UNIT = 320


SIZES = dict(
    conv_in=BASE * 27,
    bias_in=BASE,
    conv_down=WIDE * BASE * 9,
    bias_down=WIDE,
    norm_one_gain=WIDE,
    norm_one_shift=WIDE,
    conv_one=WIDE * WIDE * 9,
    bias_one=WIDE,
    time_one=FREQ * TEMB,
    time_bias_one=TEMB,
    time_two=TEMB * WIDE,
    time_bias_two=WIDE,
    norm_two_gain=WIDE,
    norm_two_shift=WIDE,
    conv_two=WIDE * WIDE * 9,
    bias_two=WIDE,
    attn_gain=WIDE,
    attn_shift=WIDE,
    attn_inner=WIDE * 3 * WIDE,
    attn_outer=WIDE * WIDE,
    attn_bias=WIDE,
    conv_up=BASE * WIDE * 9,
    bias_up=BASE,
    norm_out_gain=BASE,
    norm_out_shift=BASE,
    conv_out=3 * BASE * 9,
    bias_out=3,
)


def layout():
    return list(SIZES.items())


def start_rows():
    found = {}
    offset = 0
    for name, number in layout():
        found[name] = offset // LANES
        offset += number
    return SimpleNamespace(**found)


ROW = start_rows()
VECTOR_PLACES = dict(
    bias_in=0,
    bias_down=1,
    norm_one_gain=2,
    norm_one_shift=3,
    bias_one=4,
    time_bias_two=5,
    norm_two_gain=6,
    norm_two_shift=7,
    bias_two=8,
    attn_gain=9,
    attn_shift=10,
    attn_bias=11,
    bias_up=12,
    norm_out_gain=13,
    norm_out_shift=14,
)
VEC = SimpleNamespace(**VECTOR_PLACES)
VECTORS = [(place, getattr(ROW, name), SIZES[name] == BASE) for name, place in VECTOR_PLACES.items()]
JOINT = {(0, 0): (0,), (0, 1): (1, 2), (1, 0): (0, 1), (1, 1): (2,)}

PREP_SHAPES = dict(
    down=(3, 3 * BASE, WIDE),
    one=(3, 3 * WIDE, WIDE),
    two=(3, 3 * WIDE, WIDE),
    inner=(WIDE, 3 * WIDE),
    outer=(WIDE, WIDE),
    up=(4, 3 * WIDE, WIDE),
    time_one=(FREQ, TEMB),
    time_two=(TEMB, WIDE),
)
BACK_SHAPES = dict(
    down_t=(3, 2 * WIDE, WIDE),
    one_t=(3, 3 * WIDE, WIDE),
    two_t=(3, 3 * WIDE, WIDE),
    up_t=(4, 2 * WIDE, WIDE),
)


NN = (((1,), (0,)), ((), ()))
NT = (((1,), (1,)), ((), ()))
TN = (((0,), (0,)), ((), ()))


def product(left, right, kind):
    return lax.dot_general(left, right, kind, preferred_element_type=F32)


def dot(left, right):
    return product(left, right, NN)


def narrow_places():
    begin = 27 * lax.broadcasted_iota(jnp.int32, (32, LANES), 1)
    row = lax.broadcasted_iota(jnp.int32, (32, LANES), 0)
    low = jnp.where(begin // LANES == row, 1.0, 0.0)
    high = jnp.where(begin // LANES + 1 == row, 1.0, 0.0)
    offset = (27 * lax.broadcasted_iota(jnp.int32, (LANES, LANES), 0)) % LANES
    lane = lax.broadcasted_iota(jnp.int32, (LANES, LANES), 1)
    return low, high, offset, lane >= offset


def roll_rows(values, offset, sign):
    for bit in range(7):
        moved = pltpu.roll(values, (sign << bit) % LANES, axis=1)
        values = jnp.where((offset >> bit) % 2 == 1, moved, values)
    return values


def prep_kernel(with_back, rows, *refs):
    if rows.dtype == BF16:
        rows, low, refs = refs[-1], rows, refs[:-1]
        step = low.shape[0] // 256 * 16

        def widen(index, carry):
            block = pl.ds(pl.multiple_of(index * step, 16), step)
            rows[block, :] = low[block, :].astype(F32)
            return carry

        lax.fori_loop(0, 16, widen, 0)
        rows[16 * step :, :] = low[16 * step :, :].astype(F32)
    names = list(PREP_SHAPES) + (list(BACK_SHAPES) if with_back else [])
    out = SimpleNamespace(**dict(zip(names, refs)))
    enter, leave, bias_out, vec, bias_hidden, turned, square, taps = refs[len(names) :]

    def turn(start, wide_out, wide_in):
        count = wide_in * 9 // LANES
        for b in range(count):
            block = rows[pl.ds(start + b, wide_out, stride=count), :].T
            for c in range(0, wide_out, LANES):
                turned[c // LANES, b * LANES : (b + 1) * LANES, :] = block[:, c : c + LANES]

    def tap(k, wide_out, wide_in):
        parts = [turned[c, pl.ds(k, wide_in, stride=9), :] for c in range(wide_out // LANES)]
        return parts[0] if len(parts) == 1 else jnp.concatenate(parts, axis=1)

    for start, place, place_t in (
        (ROW.conv_one, out.one, out.one_t if with_back else None),
        (ROW.conv_two, out.two, out.two_t if with_back else None),
    ):
        turn(start, WIDE, WIDE)
        for ky in range(3):
            for kx in range(3):
                block = tap(3 * ky + kx, WIDE, WIDE)
                place[ky, kx * WIDE : (kx + 1) * WIDE, :] = block.astype(BF16)
                if with_back:
                    place_t[ky, kx * WIDE : (kx + 1) * WIDE, :] = block.T.astype(BF16)
    turn(ROW.conv_down, WIDE, BASE)
    for ky in range(3):
        for kx in range(3):
            block = tap(3 * ky + kx, WIDE, BASE)
            out.down[ky, kx * BASE : (kx + 1) * BASE, :] = block.astype(BF16)
            if with_back:
                back = block.T.astype(BF16)
                if kx == 0:
                    out.down_t[ky, 0:WIDE, BASE:] = back
                elif kx == 1:
                    out.down_t[ky, 0:WIDE, 0:BASE] = jnp.zeros((WIDE, BASE), BF16)
                    out.down_t[ky, WIDE:, 0:BASE] = back
                else:
                    out.down_t[ky, WIDE:, BASE:] = back
    turn(ROW.conv_up, BASE, WIDE)
    for py in range(2):
        for ty in range(2):
            index = 2 * py + ty
            for px in range(2):
                for tx in range(2):
                    total = None
                    for ky in JOINT[py, ty]:
                        for kx in JOINT[px, tx]:
                            term = tap(3 * ky + kx, BASE, WIDE).astype(BF16).astype(F32)
                            total = term if total is None else total + term
                    xo = px + tx
                    out.up[index, xo * WIDE : (xo + 1) * WIDE, px * BASE : (px + 1) * BASE] = (
                        total.astype(BF16)
                    )
                    if with_back:
                        at = (2 * px + tx) * BASE
                        out.up_t[index, at : at + BASE, :] = total.T.astype(BF16)
                at = 2 * WIDE if px == 0 else 0
                out.up[index, at : at + WIDE, px * BASE : (px + 1) * BASE] = jnp.zeros(
                    (WIDE, BASE), BF16
                )
    for start, place in (
        (ROW.attn_inner, out.inner),
        (ROW.attn_outer, out.outer),
        (ROW.time_one, out.time_one),
        (ROW.time_two, out.time_two),
    ):
        height, width = place.shape
        count = width // LANES
        for b in range(count):
            block = rows[pl.ds(start + b, height, stride=count), :]
            place[:, b * LANES : (b + 1) * LANES] = block.astype(BF16)
    vec[...] = jnp.zeros_like(vec)
    for place, r, narrow in VECTORS:
        second = r if narrow else r + 1
        vec[place : place + 1, 0:LANES] = rows[r : r + 1, :]
        vec[place : place + 1, LANES:] = rows[second : second + 1, :]
    for b in range(TEMB // LANES):
        r = ROW.time_bias_one + b
        bias_hidden[:, b * LANES : (b + 1) * LANES] = jnp.broadcast_to(rows[r : r + 1, :], (8, LANES))
    low, high, offset, upper_part = narrow_places()
    block = rows[0:32, :].astype(BF16)
    merged = jnp.where(
        upper_part, dot(low.T.astype(BF16), block), dot(high.T.astype(BF16), block)
    )
    merged = roll_rows(merged, offset, -1).T
    taps[...] = jnp.zeros_like(taps)
    for k in range(9):
        for c in range(3):
            taps[8 * k + c : 8 * k + c + 1, :] = merged[9 * c + k : 9 * c + k + 1, :]
    enter[...] = taps[...].astype(BF16)
    square[...] = jnp.zeros_like(square)
    for b in range(9):
        for c in range(3):
            at = ROW.conv_out + 9 * c + b
            square[c : c + 1, :] = rows[at : at + 1, :]
        turned[0, b * LANES : (b + 1) * LANES, :] = square[...].T
    for k in range(9):
        taps[8 * k : 8 * k + 8, :] = turned[0, pl.ds(k, LANES, stride=9), :].T[0:8, :]
    leave[...] = taps[...].astype(BF16)
    lane = lax.broadcasted_iota(jnp.int32, (8, LANES), 1)
    place = lax.broadcasted_iota(jnp.int32, (8, LANES), 0)
    chosen = jnp.logical_and(lane == place, place < 3)
    last = jnp.broadcast_to(rows[ROW.bias_out : ROW.bias_out + 1, :], (8, LANES))
    bias_out[...] = jnp.broadcast_to(
        jnp.sum(jnp.where(chosen, last, 0.0), axis=1, keepdims=True), (8, LANES)
    )


def prep_weights(flat, with_back):
    rows = flat.reshape(-1, LANES)
    shapes = dict(PREP_SHAPES)
    if with_back:
        shapes.update(BACK_SHAPES)
    whole = pl.BlockSpec(memory_space=pltpu.VMEM)
    made = pl.pallas_call(
        lambda *refs: prep_kernel(with_back, *refs),
        out_shape=[jax.ShapeDtypeStruct(s, BF16) for s in shapes.values()]
        + [
            jax.ShapeDtypeStruct((72, BASE), BF16),
            jax.ShapeDtypeStruct((72, BASE), BF16),
            jax.ShapeDtypeStruct((8, LANES), F32),
            jax.ShapeDtypeStruct((16, WIDE), F32),
            jax.ShapeDtypeStruct((8, TEMB), F32),
        ],
        in_specs=[whole],
        out_specs=[whole] * (len(shapes) + 5),
        scratch_shapes=[
            pltpu.VMEM((WIDE // LANES, 9 * WIDE, LANES), F32),
            pltpu.VMEM((LANES, LANES), F32),
            pltpu.VMEM((72, LANES), F32),
        ]
        + ([pltpu.VMEM(rows.shape, F32)] if rows.dtype == BF16 else []),
        compiler_params=pltpu.CompilerParams(vmem_limit_bytes=VMEM_LIMIT),
    )(rows)
    found = SimpleNamespace(**dict(zip(shapes, made)))
    found.enter, found.leave, found.bias_out, found.vec, found.bias_hidden = made[-5:]
    return found


def forward_set(found):
    return dict(
        {name: getattr(found, name) for name in PREP_SHAPES},
        vec=found.vec,
        bias_hidden=found.bias_hidden,
        enter=found.enter,
        leave=found.leave,
        bias_out=found.bias_out,
    )


def back_set(found):
    return {name: getattr(found, name) for name in BACK_SHAPES}


def move_x(values, distance):
    if distance == 0:
        return values
    column = lax.broadcasted_iota(jnp.int32, values.shape, 0) % HALF
    keep = column < HALF - 1 if distance > 0 else column >= 1
    rolled = pltpu.roll(values, (-distance) % values.shape[0], axis=0)
    return jnp.where(keep, rolled, 0.0)


def move_plane(values, ys, xs):
    if ys == 0 and xs == 0:
        return values
    lane = lax.broadcasted_iota(jnp.int32, values.shape, 1)
    row, column = lane // HALF, lane % HALF
    keep = None
    for place, step in ((row, ys), (column, xs)):
        if step:
            test = place < HALF - 1 if step > 0 else place >= 1
            keep = test if keep is None else jnp.logical_and(keep, test)
    rolled = pltpu.roll(values, (-(HALF * ys + xs)) % PIX, axis=1)
    return jnp.where(keep, rolled, 0.0)


def source_of(phase, step):
    return (phase + step) % 2, (phase + step) // 2


def silu_slope(values):
    gate = 1.0 / (1.0 + jnp.exp(-values))
    return gate * (1.0 + values * (1.0 - gate))


def silu(values):
    return values * (1.0 / (1.0 + jnp.exp(-values)))


def column_sum(values):
    return jnp.sum(values, axis=0, keepdims=True)


def group_sum(vectors, members):
    rest = 8 - len(vectors)
    stacked = jnp.concatenate(vectors + ([jnp.zeros((rest, WIDE), F32)] if rest else []), axis=0)
    high = stacked.astype(BF16).astype(F32)
    rest = stacked - high
    middle = rest.astype(BF16).astype(F32)
    parts = jnp.concatenate([high, middle, rest - middle, jnp.zeros_like(high)], axis=0)
    summed = dot(parts.astype(BF16), members[...])
    total = summed[0:8] + summed[8:16] + summed[16:24]
    return [total[i : i + 1] for i in range(len(vectors))]


NORM_WIDE = PIX * (WIDE // GROUPS)
NORM_BASE = 4 * PIX * (BASE // GROUPS)


def network_kernel(images_here, stream_count, given, made, scratch, own, *refs):
    teach, learn, r = SimpleNamespace(), SimpleNamespace(), SimpleNamespace()
    owners = [r] * len(given[0]) + [teach] * len(given[1]) + [learn] * len(given[2])
    owners += [r] * (len(made) + len(scratch))
    names = list(given[0]) + list(given[1]) + list(given[2]) + list(made) + list(scratch)
    streams = []
    for _ in range(stream_count):
        streams.append(SimpleNamespace())
        owners += [streams[-1]] * len(own)
        names += list(own)
    for owner, name, ref in zip(owners, names, refs, strict=True):
        setattr(owner, name, ref)
    wide, base = r.members_wide, r.members_base
    once = images_here == stream_count

    lane = lax.broadcasted_iota(jnp.int32, (WIDE, WIDE), 1)
    row = lax.broadcasted_iota(jnp.int32, (WIDE, WIDE), 0)
    per_wide, per_base = WIDE // GROUPS, BASE // GROUPS
    wide[...] = jnp.where(lane // per_wide == row // per_wide, 1.0, 0.0).astype(BF16)
    base[...] = jnp.where(
        (lane % BASE) // per_base == (row % BASE) // per_base, 1.0, 0.0
    ).astype(BF16)
    for q in streams:
        for ref in (q.cat_down, q.cat, q.cat_up):
            ref[...] = jnp.zeros_like(ref)
    for ref in (r.acc_vec, r.small, r.hidden_low, r.grad_shift):
        ref[...] = jnp.zeros_like(ref)
    totals = (r.acc_down, r.acc_one, r.acc_two, r.acc_up, r.acc_inner, r.acc_outer)
    if not once:
        for ref in totals + (r.grad_in, r.grad_out):
            ref[...] = jnp.zeros_like(ref)

    def vector(who, place):
        return who.vec[place : place + 1, :]

    def add_vector(place, value):
        r.acc_vec[place : place + 1, :] += value

    def time_path(who, embed, shift_ref, keep):
        pre = dot(embed[...].astype(BF16), who.time_one[...]) + who.bias_hidden[...]
        hidden = silu(pre)
        shift_ref[...] = dot(hidden.astype(BF16), who.time_two[...]) + vector(who, VEC.time_bias_two)
        if keep:
            r.hidden[...] = pre
            r.hidden_low[0:8, :] = hidden

    time_path(teach, r.embed_one, r.shift_t1, False)
    time_path(teach, r.embed_two, r.shift_t2, False)
    time_path(learn, r.embed_one, r.shift_s, True)

    def rows_product(pairs, kind=NN):
        return SimpleNamespace(answer=answer_rows, pairs=pairs, kind=kind)

    def answer_rows(asked):
        total = None
        for index, (_, right) in enumerate(asked[0].pairs):
            lefts = [ask.pairs[index][0] for ask in asked]
            left = jnp.concatenate(lefts, axis=1 if asked[0].kind is TN else 0)
            term = product(left, right[...], asked[0].kind)
            total = term if total is None else total + term
        return jnp.split(total, len(asked), axis=0)

    def lanes_product(left, right):
        return SimpleNamespace(answer=answer_lanes, left=left, right=right)

    def answer_lanes(asked):
        right = jnp.concatenate([ask.right for ask in asked], axis=0)
        return jnp.split(product(asked[0].left[...], right, NT), len(asked), axis=1)

    def add_product(target, place, left, right, kind=TN):
        return SimpleNamespace(
            answer=answer_total, target=target, place=place, left=left, right=right, kind=kind
        )

    def answer_total(asked):
        ask = asked[0]
        left = jnp.concatenate([a.left for a in asked], axis=0 if ask.kind is TN else 1)
        right = jnp.concatenate([a.right for a in asked], axis=0)
        total = product(left, right, ask.kind)
        if once:
            ask.target[ask.place] = total
        else:
            ask.target[ask.place] += total
        return [None] * len(asked)

    def group_sums(vectors, members):
        return SimpleNamespace(answer=answer_sums, vectors=vectors, members=members)

    def answer_sums(asked):
        count = len(asked[0].vectors)
        every = [vector_ for ask in asked for vector_ in ask.vectors]
        found = group_sum(every, asked[0].members)
        return [found[count * i : count * (i + 1)] for i in range(len(asked))]

    def norm_stats(blocks, members, count):
        total = sum(column_sum(block[...]) for block in blocks)
        (mean,) = yield group_sums([total], members)
        mean = mean * (1.0 / count)
        square = None
        for block in blocks:
            off = block[...] - mean
            term = column_sum(off * off)
            square = term if square is None else square + term
        (spread,) = yield group_sums([square], members)
        return mean, lax.rsqrt(spread * (1.0 / count) + 1e-05)

    def norm_back(grads, hats, gain, scale, members, count):
        plain = sum(column_sum(grad) for grad in grads)
        weighted = sum(column_sum(grad * hat) for grad, hat in zip(grads, hats))
        mean_plain, mean_weighted = yield group_sums([plain * gain, weighted * gain], members)
        mean_plain = mean_plain * (1.0 / count)
        mean_weighted = mean_weighted * (1.0 / count)
        inputs = [
            scale * (grad * gain - mean_plain - hat * mean_weighted)
            for grad, hat in zip(grads, hats)
        ]
        return inputs, weighted, plain

    def image_stream(q, index):
        taps, taps_back, first = q.taps, q.taps_back, q.first
        cat_down, cat, cat_up, joined, upper = q.cat_down, q.cat, q.cat_up, q.joined, q.upper
        body = slice(HALF, HALF + PIX)

        def set_taps(plane, sign, target):
            quarters = [plane[:, p * PIX : (p + 1) * PIX] for p in range(4)]
            for py in range(2):
                for px in range(2):
                    p = 2 * py + px
                    blocks = []
                    for ky in range(3):
                        for kx in range(3):
                            sy, ys = source_of(py, sign * (ky - 1))
                            sx, xs = source_of(px, sign * (kx - 1))
                            blocks.append(move_plane(quarters[2 * sy + sx], ys, xs))
                    target[:, p * PIX : (p + 1) * PIX] = jnp.concatenate(blocks, axis=0).astype(BF16)

        def set_cat(values):
            for kx in range(3):
                cat[body, kx * WIDE : (kx + 1) * WIDE] = move_x(values, kx - 1).astype(BF16)

        def convolve(kernel):
            return rows_product(
                [(cat[ky * HALF : ky * HALF + PIX, :], kernel.at[ky]) for ky in range(3)]
            )

        def make_plane():
            height = 3 * 2 * HALF
            rows = pl.ds(index * height, height) if isinstance(index, int) else pl.ds(
                pl.multiple_of(index * height, height), height
            )
            noisy = r.coef[index, 6] * r.images[rows, :] + r.coef[index, 7] * r.noise[rows, :]
            x = lax.broadcasted_iota(jnp.int32, (2 * HALF, 2 * PIX), 0)
            lane = lax.broadcasted_iota(jnp.int32, (2 * HALF, 2 * PIX), 1)
            spread = jnp.where(x == 2 * (lane % HALF) + lane // PIX, 1.0, 0.0).astype(BF16)
            values = dot(noisy.astype(BF16), spread)
            y = lax.broadcasted_iota(jnp.int32, values.shape, 0) % (2 * HALF)
            lane = lax.broadcasted_iota(jnp.int32, values.shape, 1) % PIX
            kept = jnp.where(lane // HALF == y // 2, values, 0.0)
            halves = []
            for py in range(2):
                part = jnp.where(y % 2 == py, kept, 0.0)
                lines = [
                    column_sum(part[c * 2 * HALF : (c + 1) * 2 * HALF, :]) for c in range(3)
                ]
                halves.append(jnp.concatenate(lines + [jnp.zeros((5, 2 * PIX), F32)], axis=0))
            return jnp.concatenate(halves, axis=1)

        def forward(who, plane, shift, keep):
            set_taps(plane, 1, taps)
            yield
            bias = vector(who, VEC.bias_in)[:, 0:BASE]
            for py in range(2):
                for px in range(2):
                    p = 2 * py + px
                    found = yield rows_product(
                        [(taps[:, p * PIX : (p + 1) * PIX], who.enter)], TN
                    )
                    first[py, :, px * BASE : (px + 1) * BASE] = found + bias
            for py in range(2):
                even, odd = first[py, :, 0:BASE], first[py, :, BASE:]
                cat_down[py, HALF:, 0:BASE] = move_x(odd, -1).astype(BF16)
                cat_down[py, HALF:, BASE : 2 * BASE] = even.astype(BF16)
                cat_down[py, HALF:, 2 * BASE :] = odd.astype(BF16)
            found = yield rows_product(
                [
                    (cat_down[1, 0:PIX, :], who.down.at[0]),
                    (cat_down[0, HALF:, :], who.down.at[1]),
                    (cat_down[1, HALF:, :], who.down.at[2]),
                ]
            )
            q.down[...] = found + vector(who, VEC.bias_down)
            stats_one = yield from norm_stats([q.down], wide, NORM_WIDE)
            hat = (q.down[...] - stats_one[0]) * stats_one[1]
            branch = silu(hat * vector(who, VEC.norm_one_gain) + vector(who, VEC.norm_one_shift))
            set_cat(branch)
            if keep:
                q.one_low[...] = branch.astype(BF16)
            found = yield convolve(who.one)
            q.branch[...] = found + (vector(who, VEC.bias_one) + shift)
            stats_two = yield from norm_stats([q.branch], wide, NORM_WIDE)
            hat = (q.branch[...] - stats_two[0]) * stats_two[1]
            branch = silu(hat * vector(who, VEC.norm_two_gain) + vector(who, VEC.norm_two_shift))
            set_cat(branch)
            if keep:
                q.two_low[...] = branch.astype(BF16)
            found = yield convolve(who.two)
            q.middle[...] = q.down[...] + found + vector(who, VEC.bias_two)
            stats_attn = yield from norm_stats([q.middle], wide, NORM_WIDE)
            hat = (q.middle[...] - stats_attn[0]) * stats_attn[1]
            tokens = hat * vector(who, VEC.attn_gain) + vector(who, VEC.attn_shift)
            tokens = tokens.astype(BF16)
            if keep:
                q.tokens[...] = tokens
            found = yield rows_product([(tokens, who.inner)])
            joined[...] = found.astype(BF16)
            scores = product(joined[:, 0:WIDE], joined[:, WIDE : 2 * WIDE], NT) * (WIDE**-0.5)
            yield
            weights = jnp.exp(scores - jnp.max(scores, axis=1, keepdims=True))
            weights = weights / jnp.sum(weights, axis=1, keepdims=True)
            if keep:
                q.soft[...] = weights
            yield
            mixed = dot(weights.astype(BF16), joined[:, 2 * WIDE :]).astype(BF16)
            if keep:
                q.mixed[...] = mixed
            found = yield rows_product([(mixed, who.outer)])
            set_cat(q.middle[...] + (found + vector(who, VEC.attn_bias)))
            for py in range(2):
                found = yield rows_product(
                    [
                        (cat[low * HALF : low * HALF + PIX, :], who.up.at[py + low])
                        for low in (py, py + 1)
                    ]
                )
                upper[py] = found + vector(who, VEC.bias_up) + first[py]
            stats_out = yield from norm_stats([upper.at[0], upper.at[1]], base, NORM_BASE)
            replies = []
            for py in range(2):
                hat = (upper[py] - stats_out[0]) * stats_out[1]
                ending = silu(
                    hat * vector(who, VEC.norm_out_gain) + vector(who, VEC.norm_out_shift)
                ).astype(BF16)
                if keep:
                    q.end[py] = ending
                for px in range(2):
                    reply = yield lanes_product(who.leave, ending[:, px * BASE : (px + 1) * BASE])
                    replies.append(reply)
            outs = []
            for py in range(2):
                for px in range(2):
                    total = None
                    for ky in range(3):
                        for kx in range(3):
                            sy, ys = source_of(py, ky - 1)
                            sx, xs = source_of(px, kx - 1)
                            k = 3 * ky + kx
                            term = move_plane(replies[2 * sy + sx][8 * k : 8 * k + 8, :], ys, xs)
                            total = term if total is None else total + term
                    outs.append(total)
            guess = jnp.concatenate(outs, axis=1) + who.bias_out[:, 0:1]
            return guess, stats_one, stats_two, stats_attn, stats_out

        def conv_back(grad, acc, value, kernel):
            for kx in range(3):
                cat[body, kx * WIDE : (kx + 1) * WIDE] = move_x(grad, 1 - kx).astype(BF16)

            def block(ky):
                low = (2 - ky) * HALF
                return cat[low : low + PIX, :]

            found = yield rows_product([(block(ky), kernel.at[ky]) for ky in range(3)])
            for ky in range(3):
                yield add_product(acc, ky, value[...], block(ky))
            return found

        def silu_norm_back(grad, place, stats, values):
            gain = vector(learn, place)
            hat = (values - stats[0]) * stats[1]
            slope = silu_slope(hat * gain + vector(learn, place + 1))
            (back,), grad_gain, grad_bias = yield from norm_back(
                [grad * slope], [hat], gain, stats[1], wide, NORM_WIDE
            )
            add_vector(place, grad_gain)
            add_vector(place + 1, grad_bias)
            return back

        at = pl.ds(index, 1)
        coef = [r.coef[index, j] for j in range(5)]
        plane = make_plane()
        guess_one = (yield from forward(teach, plane, r.shift_t1[at, :], False))[0]
        middle_state = coef[0] * guess_one + coef[1] * plane
        guess_two = (yield from forward(teach, middle_state, r.shift_t2[at, :], False))[0]
        target = coef[2] * guess_one + coef[3] * guess_two
        guess, stats_one, stats_two, stats_attn, stats_out = yield from forward(
            learn, plane, r.shift_s[at, :], True
        )
        error = guess - target
        weight = coef[4] * (1.0 / (3 * 4 * PIX))
        loss = jnp.sum(jnp.sum(error * error, axis=1, keepdims=True), axis=0, keepdims=True)
        r.small[8:9, :] += jnp.broadcast_to(loss * weight, (1, LANES))
        grad_guess = (2.0 * weight) * error
        r.small[0:8, :] += jnp.broadcast_to(
            jnp.sum(grad_guess, axis=1, keepdims=True), (8, LANES)
        )
        set_taps(grad_guess, -1, taps_back)
        yield
        grads = []
        for py in range(2):
            parts = []
            for px in range(2):
                p = 2 * py + px
                part = yield rows_product(
                    [(taps_back[:, p * PIX : (p + 1) * PIX], learn.leave)], TN
                )
                parts.append(part)
            grads.append(jnp.concatenate(parts, axis=1))
        ends = [q.end[p // 2, :, (p % 2) * BASE : (p % 2 + 1) * BASE] for p in range(4)]
        yield add_product(
            r.grad_out, slice(None), taps_back[...], jnp.concatenate(ends, axis=0), NN
        )
        gain = vector(learn, VEC.norm_out_gain)
        hats = [(upper[py] - stats_out[0]) * stats_out[1] for py in range(2)]
        shift = vector(learn, VEC.norm_out_shift)
        grads = [grad * silu_slope(hat * gain + shift) for grad, hat in zip(grads, hats)]
        grads, grad_gain, grad_bias = yield from norm_back(
            grads, hats, gain, stats_out[1], base, NORM_BASE
        )
        add_vector(VEC.norm_out_gain, grad_gain)
        add_vector(VEC.norm_out_shift, grad_bias)
        add_vector(VEC.bias_up, column_sum(grads[0]) + column_sum(grads[1]))
        for py in range(2):
            upper[py] = grads[py]
            even, odd = grads[py][:, 0:BASE], grads[py][:, BASE:]
            cat_up[py, body, 0:BASE] = move_x(even, 1).astype(BF16)
            cat_up[py, body, BASE : 2 * BASE] = even.astype(BF16)
            cat_up[py, body, 2 * BASE : 3 * BASE] = odd.astype(BF16)
            cat_up[py, body, 3 * BASE :] = move_x(odd, -1).astype(BF16)
        blocks = []
        for place in range(4):
            py, low = place // 2, (2 - place // 2 - place % 2) * HALF
            blocks.append(cat_up[py, low : low + PIX, :])
        grad_middle = yield rows_product(
            [(block, learn.up_t.at[place]) for place, block in enumerate(blocks)]
        )
        for place in range(4):
            py, low = place // 2, (2 - place // 2 - place % 2) * HALF
            yield add_product(
                r.acc_up, place, cat[body, WIDE : 2 * WIDE], cat_up[py, low : low + PIX, :]
            )
        add_vector(VEC.attn_bias, column_sum(grad_middle))
        grad_low = grad_middle.astype(BF16)
        grad_mixed = yield rows_product([(grad_low, learn.outer)], NT)
        grad_mixed = grad_mixed.astype(BF16)
        yield add_product(r.acc_outer, slice(None), q.mixed[...], grad_low)
        soft = q.soft[...]
        grad_soft = product(grad_mixed, joined[:, 2 * WIDE :], NT)
        grad_value = product(soft.astype(BF16), grad_mixed, TN)
        yield
        grad_scores = soft * (grad_soft - jnp.sum(soft * grad_soft, axis=1, keepdims=True))
        grad_scores = grad_scores.astype(BF16)
        yield
        grad_query = dot(grad_scores, joined[:, WIDE : 2 * WIDE]) * (WIDE**-0.5)
        grad_key = product(grad_scores, joined[:, 0:WIDE], TN) * (WIDE**-0.5)
        joined[:, 0:WIDE] = grad_query.astype(BF16)
        joined[:, WIDE : 2 * WIDE] = grad_key.astype(BF16)
        joined[:, 2 * WIDE :] = grad_value.astype(BF16)
        grad_tokens = yield rows_product([(joined[...], learn.inner)], NT)
        yield add_product(r.acc_inner, slice(None), q.tokens[...], joined[...])
        hat = (q.middle[...] - stats_attn[0]) * stats_attn[1]
        (back,), grad_gain, grad_bias = yield from norm_back(
            [grad_tokens], [hat], vector(learn, VEC.attn_gain), stats_attn[1], wide, NORM_WIDE
        )
        add_vector(VEC.attn_gain, grad_gain)
        add_vector(VEC.attn_shift, grad_bias)
        grad_middle = grad_middle + back
        q.middle[...] = grad_middle
        add_vector(VEC.bias_two, column_sum(grad_middle))
        grad_branch = yield from conv_back(grad_middle, r.acc_two, q.two_low, learn.two_t)
        grad_branch = yield from silu_norm_back(
            grad_branch, VEC.norm_two_gain, stats_two, q.branch[...]
        )
        bias_grad = column_sum(grad_branch)
        add_vector(VEC.bias_one, bias_grad)
        add_vector(VEC.time_bias_two, bias_grad)
        r.grad_shift[at, :] = bias_grad
        grad_branch = yield from conv_back(grad_branch, r.acc_one, q.one_low, learn.one_t)
        back = yield from silu_norm_back(grad_branch, VEC.norm_one_gain, stats_one, q.down[...])
        grad_down = q.middle[...] + back
        add_vector(VEC.bias_down, column_sum(grad_down))
        cat[0:PIX, 0:WIDE] = move_x(grad_down, 1).astype(BF16)
        cat[0:PIX, WIDE : 2 * WIDE] = grad_down.astype(BF16)
        cat[PIX : PIX + HALF, :] = jnp.zeros((HALF, 3 * WIDE), BF16)
        here, below = slice(0, PIX), slice(HALF, HALF + PIX)
        pair = slice(0, 2 * WIDE)
        even = yield rows_product([(cat[here, pair], learn.down_t.at[1])])
        odd = yield rows_product(
            [(cat[below, pair], learn.down_t.at[0]), (cat[here, pair], learn.down_t.at[2])]
        )
        grads = [even + upper[0], odd + upper[1]]
        for ky, py, rows in ((0, 1, below), (1, 0, here), (2, 1, here)):
            yield add_product(r.acc_down, ky, cat_down[py, HALF:, BASE:], cat[rows, pair])
        if not once:
            cat[0:HALF, :] = jnp.zeros((HALF, 3 * WIDE), BF16)
        add_vector(VEC.bias_in, column_sum(grads[0]) + column_sum(grads[1]))
        ends = [
            grads[p // 2][:, (p % 2) * BASE : (p % 2 + 1) * BASE].astype(BF16) for p in range(4)
        ]
        yield add_product(r.grad_in, slice(None), taps[...], jnp.concatenate(ends, axis=0), NN)

    def images_step(step, carry):
        running = [image_stream(q, step * stream_count + i) for i, q in enumerate(streams)]
        answers = [None] * stream_count
        while running:
            asked = []
            for stream, answer in zip(running, answers):
                try:
                    asked.append(stream.send(answer))
                except StopIteration:
                    pass
            if len(asked) < len(running):
                break
            if asked[0] is not None:
                answers = asked[0].answer(asked)
            else:
                answers = [None] * stream_count
        return carry

    if once:
        images_step(0, 0)
    else:
        lax.fori_loop(0, images_here // stream_count, images_step, 0)

    grad_shift = r.grad_shift[...].astype(BF16)
    grad_two = product(r.hidden_low[...].astype(BF16), grad_shift, TN)
    pre = r.hidden[...]
    grad_hidden = product(grad_shift, learn.time_two[...], NT)[0:8, :] * silu_slope(pre)
    grad_bias_hidden = column_sum(grad_hidden)
    pad = jnp.zeros((FREQ - 8, TEMB), F32)
    embed = jnp.concatenate([r.embed_one[...], pad[:, 0:FREQ]], axis=0)
    grad_one = product(
        embed.astype(BF16), jnp.concatenate([grad_hidden, pad], axis=0).astype(BF16), TN
    )

    flat, turned, square = r.flat, r.turned, r.square
    last = ROW.bias_out
    flat[last:, :] = jnp.zeros((flat.shape[0] - last, LANES), F32)
    square[...] = jnp.zeros_like(square)
    for k in range(9):
        for c in range(3):
            square[9 * c + k : 9 * c + k + 1, :] = r.grad_in[8 * k + c : 8 * k + c + 1, :]
    low, high, offset, upper_part = narrow_places()
    spread = roll_rows(square[...].T, offset, 1)
    flat[0:27, :] = (
        dot(low.astype(BF16), jnp.where(upper_part, spread, 0.0).astype(BF16))
        + dot(high.astype(BF16), jnp.where(upper_part, 0.0, spread).astype(BF16))
    )[0:27, :]
    square[...] = jnp.zeros_like(square)
    for k in range(9):
        square[0:8, :] = r.grad_out[8 * k : 8 * k + 8, :]
        turned[0, pl.ds(k, LANES, stride=9), :] = square[...].T
    for b in range(9):
        block = turned[0, b * LANES : (b + 1) * LANES, :].T
        for c in range(3):
            at = ROW.conv_out + 9 * c + b
            flat[at : at + 1, :] = block[c : c + 1, :]
    lane = lax.broadcasted_iota(jnp.int32, (8, LANES), 1)
    place = lax.broadcasted_iota(jnp.int32, (8, LANES), 0)
    flat[last : last + 1, :] = column_sum(jnp.where(lane == place, r.small[0:8, :], 0.0))
    count = r.coef[0, 5]
    for index in range(1, images_here):
        count = count + r.coef[index, 5]
    row = lax.broadcasted_iota(jnp.int32, (8, LANES), 0)
    loss = jnp.broadcast_to(r.small[8:9, :], (8, LANES))
    r.tile[...] = jnp.where(row == 0, loss, jnp.where(row == 1, count, 0.0))

    def unturn(start, wide_out, wide_in):
        count = wide_in * 9 // LANES
        for b in range(count):
            parts = [
                turned[c, b * LANES : (b + 1) * LANES, :].T for c in range(wide_out // LANES)
            ]
            block = parts[0] if len(parts) == 1 else jnp.concatenate(parts, axis=0)
            flat[pl.ds(start + b, wide_out, stride=count), :] = block

    def put_tap(k, value, wide_in):
        for c in range(0, value.shape[1], LANES):
            turned[c // LANES, pl.ds(k, wide_in, stride=9), :] = value[:, c : c + LANES]

    for start, acc in ((ROW.conv_one, r.acc_one), (ROW.conv_two, r.acc_two)):
        for ky in range(3):
            for kx in range(3):
                put_tap(3 * ky + kx, acc[ky, :, kx * WIDE : (kx + 1) * WIDE], WIDE)
        unturn(start, WIDE, WIDE)
    acc = r.acc_down
    for ky in range(3):
        put_tap(3 * ky, acc[ky, BASE:, 0:WIDE], BASE)
        put_tap(3 * ky + 1, acc[ky, 0:BASE, WIDE:], BASE)
        put_tap(3 * ky + 2, acc[ky, BASE:, WIDE:], BASE)
    unturn(ROW.conv_down, WIDE, BASE)
    acc = r.acc_up
    for ky in range(3):
        for kx in range(3):
            total = None
            for (py, ty), set_y in JOINT.items():
                for (px, tx), set_x in JOINT.items():
                    if ky in set_y and kx in set_x:
                        at = (2 * px + tx) * BASE
                        term = acc[2 * py + ty, :, at : at + BASE]
                        total = term if total is None else total + term
            put_tap(3 * ky + kx, total, WIDE)
    unturn(ROW.conv_up, BASE, WIDE)
    for start, value in (
        (ROW.attn_inner, r.acc_inner),
        (ROW.attn_outer, r.acc_outer),
        (ROW.time_one, grad_one),
        (ROW.time_two, grad_two),
    ):
        count = value.shape[1] // LANES
        for b in range(count):
            flat[pl.ds(start + b, value.shape[0], stride=count), :] = value[
                :, b * LANES : (b + 1) * LANES
            ]
    for place, at, narrow in VECTORS:
        low = r.acc_vec[place : place + 1, 0:LANES]
        high = r.acc_vec[place : place + 1, LANES:]
        if narrow:
            flat[at : at + 1, :] = low + high
        else:
            flat[at : at + 1, :] = low
            flat[at + 1 : at + 2, :] = high
    for b in range(TEMB // LANES):
        at = ROW.time_bias_one + b
        flat[at : at + 1, :] = grad_bias_hidden[:, b * LANES : (b + 1) * LANES]

    def narrow(index, carry):
        block = pl.ds(pl.multiple_of(index * UNIT, UNIT), UNIT)
        r.grad[block, :] = flat[block, :].astype(BF16)
        return carry

    lax.fori_loop(0, flat.shape[0] // UNIT, narrow, 0)


def network(images, noise, embed_one, embed_two, coef, teacher, student, row_count):
    images_here = coef.shape[0]
    whole = pl.BlockSpec(memory_space=pltpu.VMEM)
    tall = PIX + 2 * HALF
    given = (
        dict(coef=coef, images=images, noise=noise, embed_one=embed_one, embed_two=embed_two),
        forward_set(teacher),
        dict(forward_set(student), **back_set(student)),
    )
    made = dict(
        grad=((row_count, LANES), BF16),
        tile=((8, LANES), F32),
    )
    scratch = dict(
        members_wide=((WIDE, WIDE), BF16),
        members_base=((WIDE, WIDE), BF16),
        shift_t1=((8, WIDE), F32),
        shift_t2=((8, WIDE), F32),
        shift_s=((8, WIDE), F32),
        hidden=((8, TEMB), F32),
        hidden_low=((LANES, TEMB), F32),
        grad_shift=((LANES, WIDE), F32),
        acc_down=((3, WIDE, 2 * WIDE), F32),
        acc_one=((3, WIDE, 3 * WIDE), F32),
        acc_two=((3, WIDE, 3 * WIDE), F32),
        acc_up=((4, WIDE, 2 * WIDE), F32),
        acc_inner=((WIDE, 3 * WIDE), F32),
        acc_outer=((WIDE, WIDE), F32),
        acc_vec=((16, WIDE), F32),
        turned=((WIDE // LANES, 9 * WIDE, LANES), F32),
        grad_in=((72, LANES), F32),
        grad_out=((72, LANES), F32),
        small=((16, LANES), F32),
        square=((LANES, LANES), F32),
        flat=((row_count, LANES), F32),
    )
    own = dict(
        taps=((72, 4 * PIX), BF16),
        taps_back=((72, 4 * PIX), BF16),
        first=((2, PIX, WIDE), F32),
        cat_down=((2, PIX + HALF, 3 * BASE), BF16),
        cat=((tall, 3 * WIDE), BF16),
        cat_up=((2, tall, 2 * WIDE), BF16),
        down=((PIX, WIDE), F32),
        branch=((PIX, WIDE), F32),
        middle=((PIX, WIDE), F32),
        soft=((PIX, PIX), F32),
        joined=((PIX, 3 * WIDE), BF16),
        mixed=((PIX, WIDE), BF16),
        upper=((2, PIX, WIDE), F32),
        end=((2, PIX, WIDE), BF16),
        one_low=((PIX, WIDE), BF16),
        two_low=((PIX, WIDE), BF16),
        tokens=((PIX, WIDE), BF16),
    )
    stream_count = max(n for n in (4, 2, 1) if images_here % n == 0)
    arrays = [array for group in given for array in group.values()]
    specs = [whole] * len(arrays)
    specs[0] = pl.BlockSpec(memory_space=pltpu.SMEM)
    return pl.pallas_call(
        lambda *refs: network_kernel(
            images_here, stream_count, given, made, scratch, own, *refs
        ),
        out_shape=[jax.ShapeDtypeStruct(shape, kind) for shape, kind in made.values()],
        in_specs=specs,
        out_specs=[whole] * len(made),
        scratch_shapes=[
            pltpu.VMEM(shape, kind)
            for shape, kind in list(scratch.values()) + list(own.values()) * stream_count
        ],
        compiler_params=pltpu.CompilerParams(vmem_limit_bytes=VMEM_LIMIT),
    )(*arrays)


def chunk_rows(row_count, width):
    return -(-row_count // (width * UNIT)) * UNIT


def wave(times_now):
    half_freq = FREQ // 2
    freqs = jnp.exp(
        -math.log(10000.0) * jnp.arange(half_freq).astype(jnp.float32) / (half_freq - 1)
    )
    angles = 1000.0 * times_now[:, None] * freqs[None, :]
    return jnp.concatenate([jnp.sin(angles), jnp.cos(angles)], axis=1)


def local_gradient(images, noise, timesteps, counts, teacher, params, width):
    turns, slots = images.shape[0], images.shape[1]
    images_here = turns * slots
    times = (timesteps.astype(F32) / STEPS).reshape(images_here)
    times_mid = times - 0.5 / STEPS
    times_end = times - 1.0 / STEPS
    angle = 0.5 * math.pi
    alpha_now, sigma_now = jnp.cos(angle * times), jnp.sin(angle * times)
    sigma_mid, sigma_end = jnp.sin(angle * times_mid), jnp.sin(angle * times_end)
    step = math.pi / (4 * STEPS)
    slot_index = jnp.arange(slots, dtype=jnp.int32)
    valid = (slot_index[None, :] < counts[0][:, None]).astype(F32)
    weighting = valid.reshape(images_here) * (1.0 + (alpha_now / sigma_now) ** 2)
    coef = jnp.stack(
        [
            math.sin(step) / sigma_now,
            sigma_mid / sigma_now,
            sigma_end / (2.0 * math.cos(step) * sigma_mid),
            sigma_now / (2.0 * math.cos(step) * sigma_mid),
            weighting,
            valid.reshape(images_here),
            alpha_now,
            sigma_now,
        ],
        axis=1,
    )
    rows = ((0, 8 - images_here), (0, 0))
    embed_one, embed_two = jnp.pad(wave(times), rows), jnp.pad(wave(times_mid), rows)
    teacher_set = prep_weights(teacher, False)
    student_set = prep_weights(params, True)
    param_rows = params.shape[0] // LANES
    return network(
        images.reshape(-1, images.shape[-1]),
        noise.reshape(-1, noise.shape[-1]),
        embed_one,
        embed_two,
        coef,
        teacher_set,
        student_set,
        width * chunk_rows(param_rows, width),
    )


def remote(source, target, send, receive, place):
    return pltpu.make_async_remote_copy(
        src_ref=source,
        dst_ref=target,
        send_sem=send,
        recv_sem=receive,
        device_id=place,
        device_id_type=MESH,
    )


def greet(places):
    barrier = pltpu.get_barrier_semaphore()
    for place in places:
        pl.semaphore_signal(barrier, inc=1, device_id=place, device_id_type=MESH)
    pl.semaphore_wait(barrier, len(places))


def exchange_kernel(
    width, groups, param_rows, part, tile, params, first, second, whole, mean, total_tile, *rest
):
    near, partial, far, start, old_first, old_second, steps, quarter, tiles, sums = rest[0:10]
    held = rest[10:13]
    s_near, r_near, s_far, r_far, s_back, r_back, s_side, r_side = rest[13:21]
    s_tile, r_tile, s_sums, r_sums, s_step, r_step = rest[21:27]
    s_along, r_along, s_mean, r_mean, s_cross, r_cross, s_core, r_core = rest[27:35]
    chunk = part.shape[1]
    rows = chunk // PIECES
    share = chunk // groups
    share_rows = share // PIECES
    half = width // 2
    grp, me = lax.axis_index("grp"), lax.axis_index("dp")
    side, along = lax.rem(me, 2), me // 2
    beside = (grp, me + 1 - 2 * side)
    crossed = lax.rem(grp + groups // 2, groups)
    across = (crossed, me)
    twin = (grp + 1 - 2 * lax.rem(grp, 2), me)
    others = []
    for step in range(1, half):
        other = lax.rem(along + step, half)
        others.append((other, (grp, 2 * other + side)))
    peers = []
    for step in range(1, groups):
        peer = lax.rem(grp + step, groups)
        peers.append((peer, (peer, me)))
    slot = side * half + along
    mine, yours = side * half, (1 - side) * half
    greet([beside] + [place for _, place in others] + [place for _, place in peers])
    sent = []

    def send(source, target, semaphore, other_semaphore, place):
        copy = remote(source, target, semaphore, other_semaphore, place)
        copy.start()
        sent.append(copy)
        return copy

    def span(piece):
        return pl.ds(piece * rows, rows)

    first_leg = [
        send(
            part.at[pl.ds(yours, half), span(piece)],
            near.at[:, span(piece)],
            s_near.at[piece],
            r_near.at[piece],
            beside,
        )
        for piece in range(PIECES)
    ]

    full, tail = param_rows // chunk, param_rows % chunk
    pairs = ((params, start), (first, old_first), (second, old_second))

    def own_copies(count):
        at = pl.multiple_of(slot * chunk, 8)
        return [
            pltpu.make_async_copy(source.at[pl.ds(at, count)], target.at[0:count], held[i])
            for i, (source, target) in enumerate(pairs)
        ]

    for _, target in pairs:
        target[...] = jnp.zeros_like(target)

    @pl.when(slot < full)
    def _():
        copies = own_copies(chunk)
        for copy in copies:
            copy.start()
        for copy in copies:
            copy.wait()

    if tail:

        @pl.when(slot == full)
        def _():
            copies = own_copies(tail)
            for copy in copies:
                copy.start()
            for copy in copies:
                copy.wait()

    second_leg, third_leg, fourth_leg = [], [], []

    def hand_on(piece):
        first_leg[piece].wait_recv()
        partial[:, span(piece)] = (
            part[pl.ds(mine, half), span(piece)].astype(F32) + near[:, span(piece)].astype(F32)
        ).astype(BF16)
        second_leg.append(
            [
                send(
                    partial.at[other, span(piece)],
                    far.at[index, span(piece)],
                    s_far.at[piece, index],
                    r_far.at[piece, index],
                    place,
                )
                for index, (other, place) in enumerate(others)
            ]
        )

    def finish(piece):
        total = part[slot, span(piece)].astype(F32) + near[along, span(piece)].astype(F32)
        for index, copy in enumerate(second_leg[piece]):
            copy.wait_recv()
            total = total + far[index, span(piece)].astype(F32)
        low = total.astype(BF16)
        whole[slot, span(piece)] = low
        low = low.astype(F32)
        return jnp.sum((low * low).reshape(-1, 8, LANES), axis=0)

    def give_back(piece):
        here = whole.at[slot, span(piece)]
        third_leg.append(
            [
                send(here, here, s_back.at[piece, index], r_back.at[piece, index], place)
                for index, (_, place) in enumerate(others)
            ]
        )

    def pass_aside(piece):
        for copy in third_leg[piece]:
            copy.wait_recv()
        here = whole.at[pl.ds(mine, half), span(piece)]
        fourth_leg.append(send(here, here, s_side.at[piece], r_side.at[piece], beside))

    squares = None
    for step in range(PIECES + 1):
        if step < PIECES:
            hand_on(step)
        if step >= 1:
            square = finish(step - 1)
            squares = square if squares is None else squares + square

    tiles[0, 0:8, :] = squares
    tiles[0, 8:16, :] = tile[...]
    copy = send(tiles.at[0], tiles.at[1], s_tile, r_tile, beside)
    copy.wait_recv()
    sums[along] = tiles[0] + tiles[1]
    copies = [
        send(sums.at[along], sums.at[along], s_sums.at[index], r_sums.at[index], place)
        for index, (_, place) in enumerate(others)
    ]
    give_back(0)
    give_back(1)
    for copy in copies:
        copy.wait_recv()
    summed = sums[0]
    for index in range(1, half):
        summed = summed + sums[index]
    square_total = jnp.sum(jnp.sum(summed[0:8], axis=1, keepdims=True), axis=0, keepdims=True)
    valid_total = summed[9:10, 0:1]
    norm_value = jnp.sqrt(square_total) / valid_total
    factor = CLIP_NORM / jnp.maximum(norm_value, CLIP_NORM) / valid_total
    total_tile[0:8, :] = summed[8:16]
    total_tile[8:16, :] = jnp.broadcast_to(norm_value, (8, LANES))
    total_tile[16:24, :] = jnp.broadcast_to(factor, (8, LANES))

    def share_span(owner, piece):
        return pl.ds(owner * share + piece * share_rows, share_rows)

    for begin in range(0, chunk, share):
        block = slice(begin, begin + share)
        diff = adamw_update(
            whole[slot, block].astype(F32), factor, start[block], old_first[block], old_second[block]
        )[0]
        steps[block] = diff.astype(BF16)
    leaving, gathered, sided, crossed_one, crossed_two, last = [], [], [], [], [], []
    for piece in range(PIECES):
        leaving.append(
            [
                send(
                    steps.at[share_span(peer, piece)],
                    quarter.at[index, pl.ds(piece * share_rows, share_rows)],
                    s_step.at[piece, index],
                    r_step.at[piece, index],
                    place,
                )
                for index, (peer, place) in enumerate(peers)
            ]
        )

    def add_up(piece):
        total = steps[share_span(grp, piece)].astype(F32)
        for index, copy in enumerate(leaving[piece]):
            copy.wait_recv()
            total = total + quarter[index, pl.ds(piece * share_rows, share_rows)].astype(F32)
        mean[slot, share_span(grp, piece)] = (total * (1.0 / groups)).astype(BF16)
        here = mean.at[slot, share_span(grp, piece)]
        gathered.append(
            [
                send(here, here, s_along.at[piece, index], r_along.at[piece, index], place)
                for index, (_, place) in enumerate(others)
            ]
        )

    def pass_mean(piece):
        for copy in gathered[piece]:
            copy.wait_recv()
        here = mean.at[pl.ds(mine, half), share_span(grp, piece)]
        sided.append(send(here, here, s_mean.at[piece], r_mean.at[piece], beside))
        crossed_one.append(send(here, here, s_cross.at[piece, 0], r_cross.at[piece, 0], across))

    def pass_across(piece):
        sided[piece].wait_recv()
        here = mean.at[pl.ds(yours, half), share_span(grp, piece)]
        crossed_two.append(send(here, here, s_cross.at[piece, 1], r_cross.at[piece, 1], across))
        here = mean.at[:, share_span(grp, piece)]
        last.append(send(here, here, s_core.at[piece, 0], r_core.at[piece, 0], twin))

    def pass_twin(piece):
        crossed_one[piece].wait_recv()
        crossed_two[piece].wait_recv()
        here = mean.at[:, share_span(crossed, piece)]
        last.append(send(here, here, s_core.at[piece, 1], r_core.at[piece, 1], twin))

    stages = (
        (add_up, 0),
        (pass_mean, 1),
        (pass_across, 2),
        (pass_twin, 3),
    )
    for step in range(PIECES + 3):
        if step + 2 < PIECES:
            give_back(step + 2)
        if step < PIECES:
            pass_aside(step)
        for stage, lag in stages:
            if 0 <= step - lag < PIECES:
                stage(step - lag)
    for copy in fourth_leg + last:
        copy.wait_recv()
    for copy in sent:
        copy.wait_send()


def exchange(part, tile, params, first, second):
    width, groups = lax.axis_size("dp"), lax.axis_size("grp")
    rows = part.shape[0] // width
    half = width // 2
    inside = pl.BlockSpec(memory_space=pltpu.VMEM)
    outside = pl.BlockSpec(memory_space=pl.ANY)
    dma = pltpu.SemaphoreType.DMA
    many = [dma((PIECES,))] * 2
    fan = [dma((PIECES, half - 1))] * 2
    whole, mean, total = pl.pallas_call(
        lambda *refs: exchange_kernel(width, groups, params.shape[0], *refs),
        out_shape=[
            jax.ShapeDtypeStruct((width, rows, LANES), BF16),
            jax.ShapeDtypeStruct((width, rows, LANES), BF16),
            jax.ShapeDtypeStruct((24, LANES), F32),
        ],
        in_specs=[inside, inside, outside, outside, outside],
        out_specs=[inside, inside, inside],
        scratch_shapes=[
            pltpu.VMEM((half, rows, LANES), BF16),
            pltpu.VMEM((half, rows, LANES), BF16),
            pltpu.VMEM((half - 1, rows, LANES), BF16),
            pltpu.VMEM((rows, LANES), F32),
            pltpu.VMEM((rows, LANES), F32),
            pltpu.VMEM((rows, LANES), F32),
            pltpu.VMEM((rows, LANES), BF16),
            pltpu.VMEM((groups - 1, rows // groups, LANES), BF16),
            pltpu.VMEM((2, 16, LANES), F32),
            pltpu.VMEM((half, 16, LANES), F32),
        ]
        + [dma] * 3
        + many
        + fan
        + fan
        + many
        + [dma] * 2
        + [dma((half - 1,))] * 2
        + [dma((PIECES, groups - 1))] * 2
        + fan
        + many
        + [dma((PIECES, 2))] * 4,
        compiler_params=pltpu.CompilerParams(
            collective_id=1, has_side_effects=True, vmem_limit_bytes=VMEM_LIMIT
        ),
    )(part.reshape(width, rows, LANES), tile, params, first, second)
    return whole.reshape(width * rows, LANES), mean.reshape(width * rows, LANES), total


def adamw_update(gradient_sum, factor, start, first, second):
    clipped = gradient_sum * factor
    new_first = BETA_ONE * first + (1.0 - BETA_ONE) * clipped
    new_second = BETA_TWO * second + (1.0 - BETA_TWO) * clipped * clipped
    corrected = (
        new_first
        / (1.0 - BETA_ONE**STEP_COUNT)
        / (jnp.sqrt(new_second / (1.0 - BETA_TWO**STEP_COUNT)) + EPSILON)
    )
    return (RATE_INNER * (corrected + WEIGHT_DECAY * start), new_first, new_second)


def outer_step(average, start, momentum):
    new_momentum = MOMENTUM_OUTER * momentum + average
    return (start - OUTER_RATE * (average + MOMENTUM_OUTER * new_momentum), new_momentum)


def local(
    images, noise, timesteps, counts, teacher, params, first_moment, second_moment, outer_momentum
):
    width = lax.axis_size("dp")
    part, tile = local_gradient(images, noise, timesteps, counts, teacher, params, width)
    start, first, second, momentum = lax.optimization_barrier(
        tuple(
            array.reshape(-1, LANES)
            for array in (params, first_moment, second_moment, outer_momentum)
        )
    )
    total, mean, scalars = exchange(part, tile, start, first, second)
    count = start.shape[0]
    _, new_first, new_second = adamw_update(
        total[:count].astype(F32), scalars[16, 0], start, first, second
    )
    average = mean[:count].astype(F32)
    new_weights, new_outer = outer_step(average, start, momentum)
    return (
        new_weights.reshape(-1),
        new_first.reshape(1, -1),
        new_second.reshape(1, -1),
        average.reshape(-1),
        new_outer.reshape(-1),
        scalars[0, 0:1],
        scalars[1, 0:1],
        scalars[8, 0:1],
    )


def solution(mesh):
    placed = (
        P(None, ("grp", "dp"), None, None, None),
        P(None, ("grp", "dp"), None, None, None),
        P(None, ("grp", "dp")),
        P(("grp", "dp"), None),
        P(),
        P(),
        P("grp", None),
        P("grp", None),
        P(),
    )
    return jax.shard_map(
        local,
        mesh=mesh,
        in_specs=placed,
        out_specs=(P(), P("grp", None), P("grp", None), P(), P(), P("grp"), P("grp"), P("grp")),
        check_vma=False,
    )
```

profile of v0, /device:TPU:29, one launch (start us, length us, event | category | flops | bytes accessed | tf_op | source)
XLA Modules:
  0.0 296.4 jit_solution(3883097295260106471)
XLA Ops:
  0.6 0.7 fusion.8
  1.4 0.1 cos.27
  1.5 0.1 sin.77
  1.5 0.1 sin.78
  1.6 0.1 sin.79
  1.7 0.7 iota_compare_fusion.1
  2.4 0.1 lt.35
  2.5 0.7 stack.2.refs_0_
  3.2 0.1 mul.186
  3.3 0.1 mul.191
  3.4 0.1 multiply_sine_fusion
  3.5 0.7 select_maximum_fusion
  4.2 10.5 %shard_map.153 = (bf16[3,384,256]{2,1,0:T(8,128)(2,1)}, bf16[3,768,256]{2,1,0:T(8,128)(2,1)}, bf16[3,768,256]{2,1,0:T(8,128)(2,1)}, bf16[256,768]{1,0:T(8,128)(2...) custom-call(f32[17496,128]{1,0:T(8,128)} %bitcast.23), custom_call_target="tpu_custom_call" | custom-call | tf_op jit(solution)/shard_map/pallas_call | solution.py:281
  14.7 9.9 %shard_map.152 = (bf16[3,384,256]{2,1,0:T(8,128)(2,1)}, bf16[3,768,256]{2,1,0:T(8,128)(2,1)}, bf16[3,768,256]{2,1,0:T(8,128)(2,1)}, bf16[256,768]{1,0:T(8,128)(2...) custom-call(bf16[17496,128]{1,0:T(8,128)(2,1)} %bitcast.36), custom_call_target="tpu_custom_call" | custom-call | tf_op jit(solution)/shard_map/pallas_call | solution.py:281
  24.6 70.8 %shard_map.154 = (bf16[17920,128]{1,0:T(8,128)(2,1)}, f32[8,128]{1,0:T(8,128)}) custom-call(f32[4,8]{1,0:T(4,128)} %stack.2.refs_0_, f32[384,32]{1,0:T(8,128)} %bitcast.38, f32[384,32]{1,0:T(8,128)} %bitcast.39, f32[8,128]{1,0:T(8,128)} %get-tuple-element.112.refs_3_, f32[8,128]{1,0:T(8,128)} %get-tuple-element.111.refs_4_, ...), custom_call_target="tpu_custom_call" | custom-call | tf_op jit(solution)/shard_map/pallas_call | solution.py:978
  95.4 165.5 %shard_map.155 = (bf16[8,2240,128]{2,1,0:T(8,128)(2,1)}, bf16[8,2240,128]{2,1,0:T(8,128)(2,1)}, f32[24,128]{1,0:T(8,128)}) custom-call(bf16[8,2240,128]{2,1,0:T(8,128)(2,1)} %bitcast.35, f32[8,128]{1,0:T(8,128)} %get-tuple-element.79.refs_1_, f32[17496,128]{1,0:T(8,128)} %bitcast.24, f32[17496,128]{1,0:T(8,128)} %bitcast.26, f32[17496,128]{1,0:T(8,128)} %bitcast.28), custom_call_target="tpu_custom_call" | custom-call | tf_op jit(solution)/shard_map/pallas_call | solution.py:1314
  260.9 1.3 fusion.9
  262.2 0.0 copy-start
  262.2 16.1 %fusion.3 = (f32[17496,128]{1,0:T(8,128)}, f32[17496,128]{1,0:T(8,128)}) fusion(f32[17496,128]{1,0:T(8,128)} %bitcast.29, f32[]{:T(128)} %bitcast.12, bf16[17920,128]{1,0:T(8,128)(2,1)} %bitcast.37, f32[17496,128]{1,0:T(8,128)} %bitcast.27), kind=kLoop, calls=%fused_computation.7 | loop fusion | flops 20155392 | bytes 40310788 | tf_op jit(solution)/shard_map/add | solution.py:1356
  278.3 0.0 copy-done
  278.3 13.9 %fusion.4 = (f32[2239488]{0:T(1024)}, f32[2239488]{0:T(1024)}) fusion(f32[17496,128]{1,0:T(8,128)} %bitcast.32, bf16[17920,128]{1,0:T(8,128)(2,1)S(1)} %bitcast.30, f32[17496,128]{1,0:T(8,128)} %bitcast.25), kind=kLoop, calls=%fused_computation.10 | loop fusion | flops 15676416 | bytes 40310784 | tf_op jit(solution)/shard_map/reshape | solution.py:1393
  292.2 3.8 %convert_bitcast_fusion = f32[2239488]{0:T(1024)} fusion(bf16[17920,128]{1,0:T(8,128)(2,1)S(1)} %bitcast.31), kind=kLoop, calls=%fused_computation.1 | loop fusion | flops 2239488 | bytes 13436928 | tf_op jit(solution)/shard_map/reshape | solution.py:1392
  (3 shorter events, 0.0 us)
Async XLA Ops:
  262.2 16.1 %copy-start = (bf16[8,2240,128]{2,1,0:T(8,128)(2,1)S(1)}, bf16[8,2240,128]{2,1,0:T(8,128)(2,1)}, u32[]{:S(2)}) copy-start(bf16[8,2240,128]{2,1,0:T(8,128)(2,1)} %get-tuple-element.82) | copy-start | bytes 13762564
where the time goes:
time: 300 us; the launch traced here: 296 us
  Pallas kernels  257 us (86%)
  other arithmetic  36.1 us (12%)
    pallas_call x1, Pallas kernels, exchange(): pl.pallas_call(lambda *refs: exchange_kernel(width, groups, params.shape[...  166 us
    pallas_call x1, Pallas kernels, network(): pl.pallas_call(lambda *refs: network_kernel(images_here, stream_count, gi...  70.8 us
    pallas_call x2, Pallas kernels, prep_weights(): pl.pallas_call(lambda *refs: prep_kernel(with_back, *refs), out_shape=[ja...  20.4 us
    add x1, other arithmetic, adamw_update(): new_second = BETA_TWO * second + (1.0 - BETA_TWO) * clipped * clipped  16.1 us
    reshape x1, other arithmetic, local(): new_outer.reshape(-1)  13.9 us

commit v1 on v0

--- a/solution.py
+++ b/solution.py
@@ -31,6 +31,7 @@
 HALF = 16
 PIX = HALF * HALF
 VMEM_LIMIT = 60 * 1024 * 1024
+EXCHANGE_LIMIT = 26 * 1024 * 1024
 MESH = pl.DeviceIdType.MESH
 PIECES = 5
 UNIT = 320
@@ -453,7 +454,7 @@
         left = jnp.concatenate([a.left for a in asked], axis=0 if ask.kind is TN else 1)
         right = jnp.concatenate([a.right for a in asked], axis=0)
         total = product(left, right, ask.kind)
-        if once:
+        if once and ask.opens:
             ask.target[ask.place] = total
         else:
             ask.target[ask.place] += total
@@ -784,21 +785,26 @@
         yield add_product(r.grad_in, slice(None), taps[...], jnp.concatenate(ends, axis=0), NN)
 
     def images_step(step, carry):
-        running = [image_stream(q, step * stream_count + i) for i, q in enumerate(streams)]
-        answers = [None] * stream_count
-        while running:
-            asked = []
-            for stream, answer in zip(running, answers):
-                try:
-                    asked.append(stream.send(answer))
-                except StopIteration:
-                    pass
-            if len(asked) < len(running):
-                break
-            if asked[0] is not None:
-                answers = asked[0].answer(asked)
-            else:
-                answers = [None] * stream_count
+        groups = []
+        for begin in range(0, stream_count, 2):
+            members = range(begin, min(begin + 2, stream_count))
+            running = [image_stream(streams[i], step * stream_count + i) for i in members]
+            groups.append(SimpleNamespace(opens=begin == 0, running=running, answers=[None] * 2))
+        while groups:
+            for group in list(groups):
+                asked = []
+                for stream, answer in zip(group.running, group.answers):
+                    try:
+                        asked.append(stream.send(answer))
+                    except StopIteration:
+                        pass
+                if len(asked) < len(group.running):
+                    groups.remove(group)
+                elif asked[0] is None:
+                    group.answers = [None] * len(asked)
+                else:
+                    asked[0].opens = group.opens
+                    group.answers = asked[0].answer(asked)
         return carry
 
     if once:
@@ -1147,7 +1153,7 @@
             for copy in copies:
                 copy.wait()
 
-    second_leg, third_leg, fourth_leg = [], [], []
+    second_leg, third_leg, fourth_leg, squares = [], [], [], []
 
     def hand_on(piece):
         first_leg[piece].wait_recv()
@@ -1175,7 +1181,7 @@
         low = total.astype(BF16)
         whole[slot, span(piece)] = low
         low = low.astype(F32)
-        return jnp.sum((low * low).reshape(-1, 8, LANES), axis=0)
+        squares.append(jnp.sum((low * low).reshape(-1, 8, LANES), axis=0))
 
     def give_back(piece):
         here = whole.at[slot, span(piece)]
@@ -1192,61 +1198,58 @@
         here = whole.at[pl.ds(mine, half), span(piece)]
         fourth_leg.append(send(here, here, s_side.at[piece], r_side.at[piece], beside))
 
-    squares = None
-    for step in range(PIECES + 1):
-        if step < PIECES:
-            hand_on(step)
-        if step >= 1:
-            square = finish(step - 1)
-            squares = square if squares is None else squares + square
-
-    tiles[0, 0:8, :] = squares
-    tiles[0, 8:16, :] = tile[...]
-    copy = send(tiles.at[0], tiles.at[1], s_tile, r_tile, beside)
-    copy.wait_recv()
-    sums[along] = tiles[0] + tiles[1]
-    copies = [
-        send(sums.at[along], sums.at[along], s_sums.at[index], r_sums.at[index], place)
-        for index, (_, place) in enumerate(others)
-    ]
-    give_back(0)
-    give_back(1)
-    for copy in copies:
+    leaving, gathered, sided, crossed_one, crossed_two, last, tile_copies = [], [], [], [], [], [], []
+
+    def send_tiles():
+        tiles[0, 0:8, :] = sum(squares[1:], squares[0])
+        tiles[0, 8:16, :] = tile[...]
+        copy = send(tiles.at[0], tiles.at[1], s_tile, r_tile, beside)
         copy.wait_recv()
-    summed = sums[0]
-    for index in range(1, half):
-        summed = summed + sums[index]
-    square_total = jnp.sum(jnp.sum(summed[0:8], axis=1, keepdims=True), axis=0, keepdims=True)
-    valid_total = summed[9:10, 0:1]
-    norm_value = jnp.sqrt(square_total) / valid_total
-    factor = CLIP_NORM / jnp.maximum(norm_value, CLIP_NORM) / valid_total
-    total_tile[0:8, :] = summed[8:16]
-    total_tile[8:16, :] = jnp.broadcast_to(norm_value, (8, LANES))
-    total_tile[16:24, :] = jnp.broadcast_to(factor, (8, LANES))
+        sums[along] = tiles[0] + tiles[1]
+        for index, (_, place) in enumerate(others):
+            tile_copies.append(
+                send(sums.at[along], sums.at[along], s_sums.at[index], r_sums.at[index], place)
+            )
 
     def share_span(owner, piece):
         return pl.ds(owner * share + piece * share_rows, share_rows)
 
-    for begin in range(0, chunk, share):
-        block = slice(begin, begin + share)
-        diff = adamw_update(
-            whole[slot, block].astype(F32), factor, start[block], old_first[block], old_second[block]
-        )[0]
-        steps[block] = diff.astype(BF16)
-    leaving, gathered, sided, crossed_one, crossed_two, last = [], [], [], [], [], []
-    for piece in range(PIECES):
-        leaving.append(
-            [
-                send(
-                    steps.at[share_span(peer, piece)],
-                    quarter.at[index, pl.ds(piece * share_rows, share_rows)],
-                    s_step.at[piece, index],
-                    r_step.at[piece, index],
-                    place,
-                )
-                for index, (peer, place) in enumerate(peers)
-            ]
-        )
+    def step_adam():
+        for copy in tile_copies:
+            copy.wait_recv()
+        summed = sums[0]
+        for index in range(1, half):
+            summed = summed + sums[index]
+        square_total = jnp.sum(jnp.sum(summed[0:8], axis=1, keepdims=True), axis=0, keepdims=True)
+        valid_total = summed[9:10, 0:1]
+        norm_value = jnp.sqrt(square_total) / valid_total
+        factor = CLIP_NORM / jnp.maximum(norm_value, CLIP_NORM) / valid_total
+        total_tile[0:8, :] = summed[8:16]
+        total_tile[8:16, :] = jnp.broadcast_to(norm_value, (8, LANES))
+        total_tile[16:24, :] = jnp.broadcast_to(factor, (8, LANES))
+        for begin in range(0, chunk, share):
+            block = slice(begin, begin + share)
+            diff = adamw_update(
+                whole[slot, block].astype(F32),
+                factor,
+                start[block],
+                old_first[block],
+                old_second[block],
+            )[0]
+            steps[block] = diff.astype(BF16)
+        for piece in range(PIECES):
+            leaving.append(
+                [
+                    send(
+                        steps.at[share_span(peer, piece)],
+                        quarter.at[index, pl.ds(piece * share_rows, share_rows)],
+                        s_step.at[piece, index],
+                        r_step.at[piece, index],
+                        place,
+                    )
+                    for index, (peer, place) in enumerate(peers)
+                ]
+            )
 
     def add_up(piece):
         total = steps[share_span(grp, piece)].astype(F32)
@@ -1282,20 +1285,20 @@
         here = mean.at[:, share_span(crossed, piece)]
         last.append(send(here, here, s_core.at[piece, 1], r_core.at[piece, 1], twin))
 
-    stages = (
-        (add_up, 0),
-        (pass_mean, 1),
-        (pass_across, 2),
-        (pass_twin, 3),
-    )
-    for step in range(PIECES + 3):
-        if step + 2 < PIECES:
-            give_back(step + 2)
-        if step < PIECES:
-            pass_aside(step)
-        for stage, lag in stages:
-            if 0 <= step - lag < PIECES:
-                stage(step - lag)
+    h, f, g, a = hand_on, finish, give_back, pass_aside
+    u, m, x, t = add_up, pass_mean, pass_across, pass_twin
+    before = ((h, 0), (h, 1), (h, 2), (f, 0), (h, 3), (f, 1), (h, 4), (f, 2), (g, 0), (f, 3), (f, 4))
+    after = ((g, 2), (u, 0), (u, 1), (a, 1), (m, 0), (u, 2), (m, 1), (x, 0), (g, 3), (a, 2), (u, 3))
+    after += ((m, 2), (x, 1), (t, 0), (u, 4), (m, 3), (x, 2), (t, 1), (g, 4), (a, 3), (m, 4), (x, 3))
+    after += ((t, 2), (x, 4), (t, 3), (t, 4), (a, 4))
+    for stage, piece in before:
+        stage(piece)
+    send_tiles()
+    give_back(1)
+    pass_aside(0)
+    step_adam()
+    for stage, piece in after:
+        stage(piece)
     for copy in fourth_leg + last:
         copy.wait_recv()
     for copy in sent:
@@ -1344,7 +1347,7 @@
         + many
         + [dma((PIECES, 2))] * 4,
         compiler_params=pltpu.CompilerParams(
-            collective_id=1, has_side_effects=True, vmem_limit_bytes=VMEM_LIMIT
+            collective_id=1, has_side_effects=True, vmem_limit_bytes=EXCHANGE_LIMIT
         ),
     )(part.reshape(width, rows, LANES), tile, params, first, second)
     return whole.reshape(width * rows, LANES), mean.reshape(width * rows, LANES), total

time: 300 us -> 271 us (0.903)
  the two profiles are of different devices: /device:TPU:29 before, /device:TPU:0 now
where the time goes in v1:
time: 271 us; the launch traced here: 267 us
  Pallas kernels  228 us (84%)
  other arithmetic  29.4 us (11%)
  local copies, waits for them, and re-layouts  8.33 us (3%)
    pallas_call x1, Pallas kernels, exchange(): pl.pallas_call(lambda *refs: exchange_kernel(width, groups, params.shape[...  149 us
    pallas_call x1, Pallas kernels, network(): pl.pallas_call(lambda *refs: network_kernel(images_here, stream_count, gi...  58.1 us
    pallas_call x2, Pallas kernels, prep_weights(): pl.pallas_call(lambda *refs: prep_kernel(with_back, *refs), out_shape=[ja...  20.7 us
    add x1, other arithmetic, adamw_update(): new_second = BETA_TWO * second + (1.0 - BETA_TWO) * clipped * clipped  16.2 us
    reshape x1, other arithmetic, local(): new_outer.reshape(-1)  7.14 us
    unnamed x18, local copies, waits for them, and re-layouts  6.54 us

profile of v1, /device:TPU:0, one launch (start us, length us, event | category | flops | bytes accessed | tf_op | source)
XLA Modules:
  0.0 266.5 jit_solution(8512278673119853047)
XLA Ops:
  0.6 0.7 fusion.8
  1.4 0.1 cos.27
  1.5 0.1 sin.77
  1.5 0.1 sin.78
  1.6 0.1 sin.79
  1.7 0.7 iota_compare_fusion.1
  2.4 0.1 lt.35
  2.5 0.7 stack.2.refs_0_
  3.2 0.1 mul.186
  3.3 0.1 mul.191
  3.4 0.1 multiply_sine_fusion
  3.5 0.7 select_maximum_fusion
  4.2 10.5 %shard_map.153 = (bf16[3,384,256]{2,1,0:T(8,128)(2,1)}, bf16[3,768,256]{2,1,0:T(8,128)(2,1)}, bf16[3,768,256]{2,1,0:T(8,128)(2,1)}, bf16[256,768]{1,0:T(8,128)(2...) custom-call(f32[17496,128]{1,0:T(8,128)} %bitcast.23), custom_call_target="tpu_custom_call" | custom-call | tf_op jit(solution)/shard_map/pallas_call | solution.py:282
  14.7 10.2 %shard_map.152 = (bf16[3,384,256]{2,1,0:T(8,128)(2,1)}, bf16[3,768,256]{2,1,0:T(8,128)(2,1)}, bf16[3,768,256]{2,1,0:T(8,128)(2,1)}, bf16[256,768]{1,0:T(8,128)(2...) custom-call(bf16[17496,128]{1,0:T(8,128)(2,1)} %bitcast.41), custom_call_target="tpu_custom_call" | custom-call | tf_op jit(solution)/shard_map/pallas_call | solution.py:282
  24.9 58.1 %shard_map.154 = (bf16[17920,128]{1,0:T(8,128)(2,1)}, f32[8,128]{1,0:T(8,128)}) custom-call(f32[4,8]{1,0:T(4,128)} %stack.2.refs_0_, f32[384,32]{1,0:T(8,128)} %bitcast.42, f32[384,32]{1,0:T(8,128)} %bitcast.43, f32[8,128]{1,0:T(8,128)} %get-tuple-element.112.refs_3_, f32[8,128]{1,0:T(8,128)} %get-tuple-element.111.refs_4_, ...), custom_call_target="tpu_custom_call" | custom-call | tf_op jit(solution)/shard_map/pallas_call | solution.py:984
  83.1 0.0 copy-start
  83.1 3.5 %copy-done = f32[2239488]{0:T(1024)S(1)} copy-done((f32[2239488]{0:T(1024)S(1)}, f32[2239488]{0:T(1024)}, u32[]{:S(2)}) %copy-start) | copy-done | bytes 8957976
  86.6 2.3 copy-done.1
  88.9 0.7 copy-done.2
  89.6 149.1 %shard_map.155 = (bf16[8,2240,128]{2,1,0:T(8,128)(2,1)S(1)}, bf16[8,2240,128]{2,1,0:T(8,128)(2,1)S(1)}, f32[24,128]{1,0:T(8,128)S(1)}) custom-call(bf16[8,2240,128]{2,1,0:T(8,128)(2,1)S(1)} %bitcast.30, f32[8,128]{1,0:T(8,128)S(1)} %copy-done.2, f32[17496,128]{1,0:T(8,128)S(1)} %bitcast.24, f32[17496,128]{1,0:T(8,128)} %bitcast.32, f32[17496,128]{1,0:T(8,128)} %bitcast.34), custom_call_target="tpu_custom_call" | custom-call | tf_op jit(solution)/shard_map/pallas_call | solution.py:1317
  238.7 0.5 fusion.9
  239.2 16.2 %fusion.3 = (f32[17496,128]{1,0:T(8,128)}, f32[17496,128]{1,0:T(8,128)}) fusion(f32[17496,128]{1,0:T(8,128)} %bitcast.35, f32[]{:T(128)} %bitcast.12, bf16[17920,128]{1,0:T(8,128)(2,1)S(1)} %bitcast.31, f32[17496,128]{1,0:T(8,128)} %bitcast.33), kind=kLoop, calls=%fused_computation.7 | loop fusion | flops 20155392 | bytes 40310788 | tf_op jit(solution)/shard_map/add | solution.py:1359
  255.4 7.1 %fusion.4 = (f32[2239488]{0:T(1024)}, f32[2239488]{0:T(1024)}) fusion(f32[17496,128]{1,0:T(8,128)S(1)} %bitcast.38, bf16[17920,128]{1,0:T(8,128)(2,1)S(1)} %bitcast.28, f32[17496,128]{1,0:T(8,128)S(1)} %bitcast.27), kind=kLoop, calls=%fused_computation.10 | loop fusion | flops 15676416 | bytes 40310784 | tf_op jit(solution)/shard_map/reshape | solution.py:1396
  262.6 3.8 %convert_bitcast_fusion = f32[2239488]{0:T(1024)} fusion(bf16[17920,128]{1,0:T(8,128)(2,1)S(1)} %bitcast.29), kind=kLoop, calls=%fused_computation.1 | loop fusion | flops 2239488 | bytes 13436928 | tf_op jit(solution)/shard_map/reshape | solution.py:1395
  (19 shorter events, 0.0 us)
Async XLA Ops:
  83.1 3.5 %copy-start = (f32[2239488]{0:T(1024)S(1)}, f32[2239488]{0:T(1024)}, u32[]{:S(2)}) copy-start(f32[2239488]{0:T(1024)} %param.14) | copy-start | bytes 26873860
  86.6 2.3 copy-start.1
  88.9 0.7 copy-start.2
  89.6 165.8 %slice-start = ((s8[8957952]{0:T(1024)(128)(4,1)}), s8[4194304]{0:T(1024)(128)(4,1)S(1)}, s32[]{:S(2)}) async-start(s8[8957952]{0:T(1024)(128)(4,1)} %bitcast.25), calls=%async_computation | async-start | bytes 8388608
  89.6 165.8 %slice-start.1 = ((s8[8957952]{0:T(1024)(128)(4,1)}), s8[569344]{0:T(1024)(128)(4,1)S(1)}, s32[]{:S(2)}) async-start(s8[8957952]{0:T(1024)(128)(4,1)} %bitcast.25), calls=%async_computation.1 | async-start | bytes 1138688
  89.6 165.8 %slice-start.3 = ((s8[8957952]{0:T(1024)(128)(4,1)}), s8[569344]{0:T(1024)(128)(4,1)S(1)}, s32[]{:S(2)}) async-start(s8[8957952]{0:T(1024)(128)(4,1)} %bitcast.36), calls=%async_computation.3 | async-start | bytes 1138688
  89.6 165.8 %slice-start.4 = ((s8[8957952]{0:T(1024)(128)(4,1)}), s8[4194304]{0:T(1024)(128)(4,1)S(1)}, s32[]{:S(2)}) async-start(s8[8957952]{0:T(1024)(128)(4,1)} %bitcast.36), calls=%async_computation.4 | async-start | bytes 8388608
  239.2 16.2 %slice-start.2 = ((s8[8957952]{0:T(1024)(128)(4,1)}), s8[4194304]{0:T(1024)(128)(4,1)S(1)}, s32[]{:S(2)}) async-start(s8[8957952]{0:T(1024)(128)(4,1)} %bitcast.25), calls=%async_computation.2 | async-start | bytes 8388608
  239.2 16.2 %slice-start.5 = ((s8[8957952]{0:T(1024)(128)(4,1)}), s8[4194304]{0:T(1024)(128)(4,1)S(1)}, s32[]{:S(2)}) async-start(s8[8957952]{0:T(1024)(128)(4,1)} %bitcast.36), calls=%async_computation.5 | async-start | bytes 8388608
